TPU v7x, 32 devices: a whole 2x2x4 slice. The times are simulated.
32 devices in a mesh: row: 8 (over y, x, core), col: 4 (over z).
Axes of the slice: x: 2, y: 2, z: 4, core: 2. Of those that a mesh axis runs over, the one named last changes fastest.
Arguments:
- panel_block: bfloat16 [32768, 1024], P(('row', 'col')), may hold values from -1.1953125 to 1.1953125
- block_mask: int32 [256, 8], P(('row', 'col')), may hold values 0 or 1
- grid_pos: int32 [32768], P(('row', 'col')), may hold values from 0 to 32767, as said below
- lower_blocks: bfloat16 [1024, 1024], replicated, may hold values from -0.09375 to 0.09375
- diag_inv: bfloat16 [8, 128, 128], replicated, as said below
- trailing: bfloat16 [32768, 16384], P('row', 'col'), may hold values from -6 to 6
Outputs:
- factor: bfloat16 [32768, 1024], P(('row', 'col'))
- complement: bfloat16 [32768, 16384], P('row', 'col')
Inputs may be any that keep to these rules, and one draw needn't show every extreme that they name: grid_pos is a permutation; every aligned block of 1024 entries holds exactly 128 values in each range [r * 4096, (r + 1) * 4096). Each diag_inv[j] is lower triangular.
All inputs are finite; a program needn't handle non-finite values. No bound on the sum of `block_mask` on one device may be relied on, other than what follows from the above.
Results may differ from a plain program's by a relative error of at most 0.0061.
Values may be sent and summed in bfloat16 or wider, within the bound.
A program may use at most 128 MiB of HBM per device.

v0:
```python
import jax
import jax.numpy as jnp
from jax import lax
from jax.sharding import PartitionSpec as P


def broadcast(block, axis, source):
    block = jnp.where(lax.axis_index(axis) == source, block, jnp.zeros_like(block))
    return lax.psum(block, axis)


def apply_mask(panel_block, block_mask, block_width):
    row_blocks = panel_block.shape[0] // block_width
    shaped = panel_block.reshape(row_blocks, block_width, block_mask.shape[1], block_width)
    keeping = (block_mask > 0)[:, None, :, None]
    return jnp.where(keeping, shaped, jnp.zeros_like(shaped)).reshape(panel_block.shape)


def solve_panel(masked, lower_blocks, diag_inv):
    block_width = diag_inv.shape[1]
    solved = []
    for block_index in range(diag_inv.shape[0]):
        offset = block_index * block_width
        current = masked[:, offset : offset + block_width].astype(jnp.float32)
        if block_index > 0:
            earlier = jnp.concatenate(solved, axis=1)
            current = current - lax.dot_general(
                earlier,
                lower_blocks[offset : offset + block_width, :offset],
                (((1,), (1,)), ((), ())),
                preferred_element_type=jnp.float32,
            )
        residue = current.astype(jnp.bfloat16)
        solved.append(
            lax.dot_general(
                residue,
                diag_inv[block_index],
                (((1,), (1,)), ((), ())),
                preferred_element_type=jnp.float32,
            ).astype(jnp.bfloat16)
        )
    return jnp.concatenate(solved, axis=1)


def arrange(values, positions, base_pos):
    return values[jnp.argsort(positions - base_pos)]


def local(panel_block, block_mask, grid_pos, lower_blocks, diag_inv, trailing):
    block_width = diag_inv.shape[1]
    masked = apply_mask(panel_block, block_mask, block_width)
    factor = solve_panel(masked, lower_blocks, diag_inv)
    columns = factor.shape[1]
    grid_rows = trailing.shape[0]
    row_count = lax.axis_size("row")
    per_row = panel_block.shape[0] // row_count
    by_grid = jnp.argsort(grid_pos)
    grouped = factor[by_grid].reshape(row_count, per_row, columns)
    grouped_pos = grid_pos[by_grid].reshape(row_count, per_row)
    arrived, arrived_pos = (
        lax.all_to_all(grouped, "row", split_axis=0, concat_axis=0, tiled=True),
        lax.all_to_all(grouped_pos, "row", split_axis=0, concat_axis=0, tiled=True),
    )
    gathered, gathered_pos = (
        lax.all_gather(arrived.reshape(-1, columns), "col", axis=0, tiled=True),
        lax.all_gather(arrived_pos.reshape(-1), "col", axis=0, tiled=True),
    )
    row_part = arrange(gathered, gathered_pos, lax.axis_index("row") * grid_rows)
    column_part = broadcast(row_part, "row", lax.axis_index("col"))
    product = lax.dot_general(
        row_part, column_part, (((1,), (1,)), ((), ())), preferred_element_type=jnp.float32
    )
    complement = (trailing.astype(jnp.float32) - product).astype(jnp.bfloat16)
    return (factor, complement)


def solution(mesh):
    placed = (
        P(("row", "col"), None),
        P(("row", "col"), None),
        P(("row", "col")),
        P(),
        P(),
        P("row", "col"),
    )
    return jax.shard_map(
        local,
        mesh=mesh,
        in_specs=placed,
        out_specs=(P(("row", "col"), None), P("row", "col")),
        check_vma=False,
    )
```

profile of v0, /device:TPU:0, one launch (start us, length us, event | category | flops | bytes accessed | tf_op | source)
XLA Modules:
  0.0 433.3 jit_solution(4966387108954403292)
XLA Ops:
  7.2 0.0 all-gather.2.cloned.1.call-start
  7.2 0.7 broadcast_compare_fusion
  7.9 5.1 %sort.34 = (s32[1024]{0:T(1024)}, s32[1024]{0:T(1024)S(1)}) sort(s32[1024]{0:T(1024)} %param.8, s32[1024]{0:T(1024)S(1)} %iota.8), dimensions={0}, to_apply=%region_0.1 | sort | flops 10240 | bytes 16384 | tf_op jit(solution)/shard_map/jit(argsort)/sort | solution.py:57
  13.0 0.3 broadcast_in_dim.24
  13.3 0.0 copy-start.2
  13.3 2.2 bitcast_select_fusion
  15.5 0.0 copy-done.2
  15.5 1.2 constant_dynamic-update-slice_fusion.17
  16.8 2.3 constant_dynamic-update-slice_fusion.16
  19.0 2.4 constant_dynamic-update-slice_fusion.15
  21.4 2.5 constant_dynamic-update-slice_fusion.14
  23.9 2.6 constant_dynamic-update-slice_fusion.13
  26.5 3.0 constant_dynamic-update-slice_fusion.12
  29.4 3.0 constant_dynamic-update-slice_fusion.11
  32.4 3.1 fusion.6
  35.5 2.9 copy.13
  38.4 0.0 copy-start.1
  38.4 5.3 %gather_fusion = bf16[1024,1024]{1,0:T(8,128)(2,1)} fusion(bf16[1024,1024]{1,0:T(8,128)(2,1)S(1)} %copy.13, s32[1024]{0:T(1024)S(1)} %fusion.84), kind=kCustom, calls=%fused_computation | custom fusion | bytes 4198400 | tf_op jit(solution)/shard_map/gather | solution.py:58
  43.7 0.0 copy-done.1
  43.7 31.9 %all_to_all.14 = bf16[8,128,1024]{2,1,0:T(8,128)(2,1)} all-to-all(bf16[8,128,1024]{2,1,0:T(8,128)(2,1)} %bitcast.52), channel_id=1, replica_groups=mesh['row'=8,'col'=4] {'row'}, dimensions={0} | all-to-all | bytes 4194304 | tf_op jit(solution)/shard_map/all_to_all | solution.py:61
  75.6 0.0 copy-start
  75.6 0.0 all-gather.2.cloned.1.call-update
  75.6 0.7 copy-done
  76.3 8.8 %gather_fusion.1 = s32[1024]{0:T(1024)} fusion(s32[1024]{0:T(1024)S(1)} %copy-done, s32[1024]{0:T(1024)S(1)} %fusion.84), kind=kCustom, calls=%fused_computation.1 | custom fusion | bytes 12288 | tf_op jit(solution)/shard_map/gather | solution.py:59
  85.1 3.3 all-to-all-start.1
  88.5 0.0 all-reduce.2.cloned.1.call-start
  88.5 4.5 %all-to-all-done.1 = s32[8,1,128]{2,1,0:T(1,128)S(1)} async-done(((s32[8,1,128]{2,1,0:T(1,128)}), s32[8,1,128]{2,1,0:T(1,128)S(1)}, u32[]{:S(2)}, u32[]{:S(2)}) %all-to-all-start.1) | async-done | bytes 4128 | tf_op jit(solution)/shard_map/all_to_all | solution.py:62
  93.0 19.6 %all_gather.7 = s32[4096]{0:T(1024)S(1)} all-gather(s32[1024]{0:T(1024)S(1)} %bitcast.55), channel_id=1, replica_groups=mesh['row'=8,'col'=4] {'col'}, dimensions={0}, use_global_device_ids=true | all-gather | bytes 20480 | tf_op jit(solution)/shard_map/all_gather | solution.py:66
  112.6 5.8 %sort.35 = (s32[4096]{0:T(1024)}, s32[4096]{0:T(1024)S(1)}) sort(s32[4096]{0:T(1024)S(1)} %broadcast_subtract_fusion, s32[4096]{0:T(1024)S(1)} %iota.9), dimensions={0}, to_apply=%region_1.2 | sort | flops 49152 | bytes 65536 | tf_op jit(solution)/shard_map/jit(argsort)/sort | solution.py:46
  118.4 107.2 %all-gather.2.cloned.1.call-done = bf16[4096,1024]{1,0:T(8,128)(2,1)} async-done(((bf16[1024,1024]{1,0:T(8,128)(2,1)}), bf16[4096,1024]{1,0:T(8,128)(2,1)}) %all-gather.2.cloned.1.call-update) | async-done | bytes 8388624 | tf_op jit(solution)/shard_map/all_gather | solution.py:65
  225.5 25.3 %gather_fusion.2 = bf16[4096,1024]{1,0:T(8,128)(2,1)} fusion(bf16[4096,1024]{1,0:T(8,128)(2,1)} %all-gather.2.cloned.1.call-done, s32[4096]{0:T(1024)S(1)} %fusion.83), kind=kCustom, calls=%fused_computation.2 | custom fusion | bytes 16793600 | tf_op jit(solution)/shard_map/gather | solution.py:46
  250.9 7.3 %broadcast_select_fusion = bf16[4096,1024]{1,0:T(8,128)(2,1)} fusion(bf16[4096,1024]{1,0:T(8,128)(2,1)} %gather_fusion.2, pred[]{:T(512)S(6)} %eq.3), kind=kLoop, calls=%fused_computation.4 | loop fusion | flops 4194304 | bytes 16777216 | tf_op jit(solution)/shard_map/jit(_where)/select_n | solution.py:8
  258.2 0.0 all-reduce.2.cloned.1.call-update
  258.2 124.1 %all-reduce.2.cloned.1.call-done = bf16[4096,1024]{1,0:T(8,128)(2,1)} async-done(((bf16[4096,1024]{1,0:T(8,128)(2,1)}), bf16[4096,1024]{1,0:T(8,128)(2,1)}) %all-reduce.2.cloned.1.call-update) | async-done | bytes 8388624 | tf_op jit(solution)/shard_map/psum | solution.py:9
  382.3 44.1 %subtract_convert_fusion = bf16[4096,4096]{1,0:T(8,128)(2,1)} fusion(bf16[4096,4096]{1,0:T(8,128)(2,1)} %param.11, bf16[4096,1024]{1,0:T(8,128)(2,1)} %gather_fusion.2, bf16[4096,1024]{1,0:T(8,128)(2,1)} %all-reduce.2.cloned.1.call-done), kind=kOutput, calls=%fused_computation.3 | convolution fusion | flops 34410070016 | bytes 83886080 | tf_op jit(solution)/shard_map/dot_general | solution.py:70
  (5 shorter events, 0.0 us)
Async XLA Ops:
  7.2 218.4 %all-gather.2.cloned.1.call-start = ((), (), s32[]{:S(2)}) async-start(), calls=%async_computation.2 | async-start | bytes 10485760 | tf_op jit(solution)/shard_map/all_gather | solution.py:65
  13.3 2.2 copy-start.2
  38.4 5.4 %copy-start.1 = (bf16[1024,1024]{1,0:T(8,128)(2,1)}, bf16[1024,1024]{1,0:T(8,128)(2,1)S(1)}, u32[]{:S(2)}) copy-start(bf16[1024,1024]{1,0:T(8,128)(2,1)S(1)} %copy.13) | copy-start | bytes 6291460
  75.6 0.7 copy-start
  85.1 7.8 %all-to-all-start.1 = ((s32[8,1,128]{2,1,0:T(1,128)}), s32[8,1,128]{2,1,0:T(1,128)S(1)}, u32[]{:S(2)}, u32[]{:S(2)}) async-start(s32[8,1,128]{2,1,0:T(1,128)} %bitcast.10), calls=%async_computation.1 | async-start | bytes 8192 | tf_op jit(solution)/shard_map/all_to_all | solution.py:62
  88.5 293.9 %all-reduce.2.cloned.1.call-start = ((), (), s32[]{:S(2)}) async-start(), calls=%async_computation.3 | async-start | bytes 16777216 | tf_op jit(solution)/shard_map/psum | solution.py:9
Sparse Core Ops, SparseCore 0:
  75.8 149.7 all-gather.1
  258.3 123.9 all-reduce.1
where the time goes:
time: 434 us; the launch traced here: 433 us
  waiting for transfers between devices  236 us (54%)
  matrix products  64.1 us (15%)
  blocking collectives  51.5 us (12%)
  local copies, waits for them, and re-layouts  43.4 us (10%)
  other arithmetic  21.1 us (5%)
  between operations  14.1 us (3%)
    psum x1, waiting for transfers between devices, broadcast(): return lax.psum(block, axis)  124 us
    all_gather x1, waiting for transfers between devices, local(): lax.all_gather(arrived.reshape(-1, columns), 'col', axis=0, tiled=True)  107 us
    dot_general x1, matrix products, local(): lax.dot_general(row_part, column_part, (((1,), (1,)), ((), ())), preferre...  44.1 us
    all_to_all x1, blocking collectives, local(): lax.all_to_all(grouped, 'row', split_axis=0, concat_axis=0, tiled=True)  31.9 us
    gather x1, local copies, waits for them, and re-layouts, arrange(): return values[jnp.argsort(positions - base_pos)]  25.3 us
    dot_general x8, matrix products, solve_panel(): lax.dot_general(residue, diag_inv[block_index], (((1,), (1,)), ((), ())),...  20 us
    all_gather x1, blocking collectives, local(): lax.all_gather(arrived_pos.reshape(-1), 'col', axis=0, tiled=True)  19.6 us
    gather x1, local copies, waits for them, and re-layouts, local(): grouped_pos = grid_pos[by_grid].reshape(row_count, per_row)  8.83 us
  transfers between devices with their start and end apart: 3, of which 3 were waited for; matrix products, arithmetic and copies ran while one was open for 3% of the time, Pallas kernels for 0%

commit v1 on v0

v1 whole, which is shorter than its diff:
```python
import functools

import jax
import jax.numpy as jnp
from jax import lax
from jax.experimental import pallas as pl
from jax.experimental.pallas import tpu as pltpu
from jax.sharding import PartitionSpec as P

PIECES = 4
EARLY = 3
TRANSPOSED = (((1,), (1,)), ((), ()))


def apply_mask(panel_block, block_mask, block_width):
    row_blocks = panel_block.shape[0] // block_width
    shaped = panel_block.reshape(row_blocks, block_width, block_mask.shape[1], block_width)
    keeping = (block_mask > 0)[:, None, :, None]
    return jnp.where(keeping, shaped, jnp.zeros_like(shaped)).reshape(panel_block.shape)


def solve_block(masked, solved, lower_blocks, diag_inv, block_index):
    block_width = diag_inv.shape[1]
    offset = block_index * block_width
    current = masked[:, offset : offset + block_width].astype(jnp.float32)
    if block_index > 0:
        earlier = jnp.concatenate(solved, axis=1)
        current = current - lax.dot_general(
            earlier,
            lower_blocks[offset : offset + block_width, :offset],
            TRANSPOSED,
            preferred_element_type=jnp.float32,
        )
    residue = current.astype(jnp.bfloat16)
    return lax.dot_general(
        residue, diag_inv[block_index], TRANSPOSED, preferred_element_type=jnp.float32
    ).astype(jnp.bfloat16)


def take_rows(values, order):
    return values.at[order].get(mode="promise_in_bounds", unique_indices=True)


def update_kernel(pieces, *refs):
    left, right = refs[:pieces], refs[pieces : 2 * pieces]
    base_ref, out_ref = refs[2 * pieces], refs[2 * pieces + 1]
    total = None
    for one, other in zip(left, right):
        product = lax.dot_general(
            one[...], other[...], TRANSPOSED, preferred_element_type=jnp.float32
        )
        total = product if total is None else total + product
    out_ref[...] = (base_ref[...].astype(jnp.float32) - total).astype(out_ref.dtype)


def update(left, right, base, in_place):
    pieces = len(left)
    rows, columns = base.shape
    depth = left[0].shape[1]
    tile_m, tile_n = min(512, rows), min(1024, columns)
    spec_left = pl.BlockSpec((tile_m, depth), lambda j, i: (i, 0))
    spec_right = pl.BlockSpec((tile_n, depth), lambda j, i: (j, 0))
    spec_out = pl.BlockSpec((tile_m, tile_n), lambda j, i: (i, j))
    return pl.pallas_call(
        functools.partial(update_kernel, pieces),
        grid=(columns // tile_n, rows // tile_m),
        out_shape=jax.ShapeDtypeStruct(base.shape, base.dtype),
        in_specs=[spec_left] * pieces + [spec_right] * pieces + [spec_out],
        out_specs=spec_out,
        input_output_aliases={2 * pieces: 0} if in_place else {},
        compiler_params=pltpu.CompilerParams(vmem_limit_bytes=40 * 1024 * 1024),
        cost_estimate=pl.CostEstimate(
            flops=2 * rows * columns * depth * pieces,
            bytes_accessed=4 * rows * columns,
            transcendentals=0,
        ),
    )(*left, *right, base)


def local(panel_block, block_mask, grid_pos, lower_blocks, diag_inv, trailing):
    blocks, block_width = diag_inv.shape[0], diag_inv.shape[1]
    rows_dev = panel_block.shape[0]
    grid_rows = trailing.shape[0]
    n_row, n_col = lax.axis_size("row"), lax.axis_size("col")
    slot = rows_dev // n_row
    me_row, me_col = lax.axis_index("row"), lax.axis_index("col")

    sorted_pos, by_grid = lax.sort(
        (grid_pos, lax.iota(jnp.int32, rows_dev)), num_keys=1, is_stable=False
    )
    all_pos = lax.all_gather(sorted_pos, ("row", "col"), axis=0, tiled=False)
    all_pos = all_pos.reshape(n_row, n_col, n_row, slot)
    pos_row = lax.dynamic_index_in_dim(all_pos, me_row, 2, keepdims=False)
    pos_col = lax.dynamic_index_in_dim(all_pos, me_col, 2, keepdims=False)
    keys = jnp.stack([pos_row.transpose(1, 0, 2).reshape(-1), pos_col.reshape(-1)])
    _, orders = lax.sort(
        (keys, lax.broadcasted_iota(jnp.int32, keys.shape, 1)),
        dimension=1,
        num_keys=1,
        is_stable=False,
    )
    order_row, order_col = orders[0], orders[1]

    masked = apply_mask(panel_block, block_mask, block_width)
    solved, row_parts, column_parts = [], [], []
    per_piece = blocks // PIECES
    for piece in range(PIECES):
        for block_index in range(piece * per_piece, (piece + 1) * per_piece):
            solved.append(solve_block(masked, solved, lower_blocks, diag_inv, block_index))
        mine = jnp.concatenate(solved[-per_piece:], axis=1)
        width = mine.shape[1]
        grouped = take_rows(mine, by_grid).reshape(n_row, slot, width)
        arrived = lax.all_to_all(grouped, "row", split_axis=0, concat_axis=0, tiled=True)
        gathered = lax.all_gather(arrived.reshape(-1, width), "col", axis=0, tiled=True)
        row_parts.append(take_rows(gathered, order_row))
        across = lax.all_to_all(grouped[:n_col], "col", split_axis=0, concat_axis=0, tiled=True)
        beside = lax.all_gather(across.reshape(-1, width), "row", axis=0, tiled=True)
        column_parts.append(take_rows(beside, order_col))
    factor = jnp.concatenate(solved, axis=1)
    partial = update(row_parts[:EARLY], column_parts[:EARLY], trailing, False)
    complement = update(row_parts[EARLY:], column_parts[EARLY:], partial, True)
    return (factor, complement)


def solution(mesh):
    placed = (
        P(("row", "col"), None),
        P(("row", "col"), None),
        P(("row", "col")),
        P(),
        P(),
        P("row", "col"),
    )
    return jax.shard_map(
        local,
        mesh=mesh,
        in_specs=placed,
        out_specs=(P(("row", "col"), None), P("row", "col")),
        check_vma=False,
    )
```

time: 434 us -> 537 us (1.24)
  waiting for transfers between devices: 236 us -> 44.2 us
  local copies, waits for them, and re-layouts: 43.4 us -> 175 us
  blocking collectives: 51.5 us -> 176 us
  Pallas kernels: 0 us -> 85.1 us
  matrix products: 64.1 us -> 21 us
  other arithmetic: 21.1 us -> 10.8 us
    psum x1 -> x0, waiting for transfers between devices: 124 us -> none  [broadcast(): return lax.psum(block, axis)]
    gather x3 -> x12, local copies, waits for them, and re-layouts: 39.5 us -> 156 us  [take_rows(): return values.at[order].get(mode='promise_in_bounds', unique_indices=True)]
    pallas_call x0 -> x2, Pallas kernels: none -> 85.1 us  [update(): pl.pallas_call(functools.partial(update_kernel, pieces), grid=(columns //...]
    all_to_all x0 -> x4, blocking collectives: none -> 67.5 us  [local(): lax.all_to_all(grouped[:n_col], 'col', split_axis=0, concat_axis=0, tiled...]
    all_gather x1 -> x8, waiting for transfers between devices: 107 us -> 44 us  [the longest x4 35 us: local(): lax.all_gather(across.reshape(-1, width), 'row', axis=0, tiled=True)]
    all_gather x1, blocking collectives: 19.6 us -> 70 us  [local(): all_pos = lax.all_gather(sorted_pos, ('row', 'col'), axis=0, tiled=False)]
    dot_general x9 -> x8, matrix products: 64.1 us -> 21 us  [solve_block(): lax.dot_general(residue, diag_inv[block_index], TRANSPOSED, preferred_ele...]
    unnamed x7 -> x26, local copies, waits for them, and re-layouts: 3.53 us -> 16.3 us
  transfers between devices with their start and end apart: 3 -> 9, of which waited for: 3 -> 4; matrix products, arithmetic and copies ran while one was open for 3% -> 29% of each run, Pallas kernels for 0% -> 8%
where the time goes in v1:
time: 537 us; the launch traced here: 533 us
  blocking collectives  176 us (33%)
  local copies, waits for them, and re-layouts  175 us (33%)
  Pallas kernels  85.1 us (16%)
  waiting for transfers between devices  44.2 us (8%)
  matrix products  21 us (4%)
  between operations  15.8 us (3%)
  other arithmetic  10.8 us (2%)
  starting transfers between devices  5.53 us (1%)
    gather x12, local copies, waits for them, and re-layouts, take_rows(): return values.at[order].get(mode='promise_in_bounds', unique_indices=True)  156 us
    pallas_call x2, Pallas kernels, update(): pl.pallas_call(functools.partial(update_kernel, pieces), grid=(columns //...  85.1 us
    all_gather x1, blocking collectives, local(): all_pos = lax.all_gather(sorted_pos, ('row', 'col'), axis=0, tiled=False)  70 us
    all_to_all x4, blocking collectives, local(): lax.all_to_all(grouped[:n_col], 'col', split_axis=0, concat_axis=0, tiled...  67.5 us
    all_to_all x3, blocking collectives, local(): lax.all_to_all(grouped, 'row', split_axis=0, concat_axis=0, tiled=True)  38.5 us
    all_gather x4, waiting for transfers between devices, local(): lax.all_gather(across.reshape(-1, width), 'row', axis=0, tiled=True)  35 us
    dot_general x8, matrix products, solve_block(): lax.dot_general(residue, diag_inv[block_index], TRANSPOSED, preferred_ele...  21 us
    unnamed x26, local copies, waits for them, and re-layouts  16.3 us
  transfers between devices with their start and end apart: 9, of which 4 were waited for; matrix products, arithmetic and copies ran while one was open for 29% of the time, Pallas kernels for 8%

profile of v1, /device:TPU:0, one launch (start us, length us, event | category | flops | bytes accessed | tf_op | source)
XLA Modules:
  0.0 533.0 jit_solution(2381249600797767216)
XLA Ops:
  8.7 4.3 sort.30
  13.4 2.2 bitcast_select_fusion
  15.6 1.2 constant_dynamic-update-slice_fusion.17
  16.8 2.3 constant_dynamic-update-slice_fusion.16
  19.1 2.5 constant_dynamic-update-slice_fusion.15
  21.5 2.7 constant_dynamic-update-slice_fusion.14
  24.2 1.0 pad_maximum_fusion.2
  25.4 4.9 gather_fusion.5
  30.3 5.2 all-to-all-start.3
  35.6 70.0 %all-gather = s32[32768]{0:T(1024)S(1)} all-gather(s32[1024]{0:T(1024)S(1)} %get-tuple-element.6), channel_id=2, replica_groups=mesh['row'=8,'col'=4] {'row','col'}, dimensions={0}, use_global_device_ids=true | all-gather | bytes 135168 | tf_op jit(solution)/shard_map/all_gather | solution.py:91
  107.8 1.0 pad_maximum_fusion
  109.0 3.9 gather_fusion.3
  112.9 12.8 %all_to_all.40 = bf16[8,128,256]{2,1,0:T(8,128)(2,1)} all-to-all(bf16[8,128,256]{2,1,0:T(8,128)(2,1)S(1)} %bitcast.78), channel_id=1, replica_groups=mesh['row'=8,'col'=4] {'row'}, dimensions={0} | all-to-all | bytes 1048576 | tf_op jit(solution)/shard_map/all_to_all | solution.py:113
  125.8 2.9 constant_dynamic-update-slice_fusion.13
  128.7 3.1 constant_dynamic-update-slice_fusion.12
  131.8 3.1 constant_dynamic-update-slice_fusion.11
  134.9 3.2 constant_dynamic-update-slice_fusion.18
  138.4 3.9 gather_fusion
  142.4 12.8 %all_to_all.41 = bf16[8,128,256]{2,1,0:T(8,128)(2,1)} all-to-all(bf16[8,128,256]{2,1,0:T(8,128)(2,1)S(1)} %bitcast.79), channel_id=1, replica_groups=mesh['row'=8,'col'=4] {'row'}, dimensions={0} | all-to-all | bytes 1048576 | tf_op jit(solution)/shard_map/all_to_all | solution.py:113
  155.6 3.9 gather_fusion.7
  159.5 12.8 %all_to_all.42 = bf16[8,128,256]{2,1,0:T(8,128)(2,1)} all-to-all(bf16[8,128,256]{2,1,0:T(8,128)(2,1)S(1)} %bitcast.80), channel_id=1, replica_groups=mesh['row'=8,'col'=4] {'row'}, dimensions={0} | all-to-all | bytes 1048576 | tf_op jit(solution)/shard_map/all_to_all | solution.py:113
  172.4 19.8 %all_to_all.43 = bf16[4,128,256]{2,1,0:T(8,128)(2,1)} all-to-all(bf16[4,128,256]{2,1,0:T(8,128)(2,1)S(1)} %bitcast.89), channel_id=1, replica_groups=mesh['row'=8,'col'=4] {'col'}, dimensions={0} | all-to-all | bytes 524288 | tf_op jit(solution)/shard_map/all_to_all | solution.py:116
  192.4 1.0 slice.166
  193.3 14.4 %all_to_all.44 = bf16[4,128,256]{2,1,0:T(8,128)(2,1)} all-to-all(bf16[4,128,256]{2,1,0:T(8,128)(2,1)S(1)} %bitcast.90), channel_id=1, replica_groups=mesh['row'=8,'col'=4] {'col'}, dimensions={0} | all-to-all | bytes 524288 | tf_op jit(solution)/shard_map/all_to_all | solution.py:116
  207.9 12.1 %all_to_all.45 = bf16[4,128,256]{2,1,0:T(8,128)(2,1)} all-to-all(bf16[4,128,256]{2,1,0:T(8,128)(2,1)S(1)} %bitcast.91), channel_id=1, replica_groups=mesh['row'=8,'col'=4] {'col'}, dimensions={0} | all-to-all | bytes 524288 | tf_op jit(solution)/shard_map/all_to_all | solution.py:116
  220.0 21.1 %all_to_all.46 = bf16[4,128,256]{2,1,0:T(8,128)(2,1)} all-to-all(bf16[4,128,256]{2,1,0:T(8,128)(2,1)S(1)} %bitcast.92), channel_id=1, replica_groups=mesh['row'=8,'col'=4] {'col'}, dimensions={0} | all-to-all | bytes 524288 | tf_op jit(solution)/shard_map/all_to_all | solution.py:116
  241.2 3.9 copy.36
  246.1 17.7 %gather_fusion.6 = bf16[4096,256]{1,0:T(8,128)(2,1)} fusion(bf16[4096,256]{1,0:T(8,128)(2,1)} %all-gather.16.cloned.1.call-done, s32[4096]{0:T(1024)S(1)} %get-tuple-element.57), kind=kCustom, calls=%fused_computation.6 | custom fusion | bytes 4210688 | tf_op jit(solution)/shard_map/gather | solution.py:41
  263.8 17.8 %gather_fusion.4 = bf16[4096,256]{1,0:T(8,128)(2,1)} fusion(bf16[4096,256]{1,0:T(8,128)(2,1)} %all-gather.14.cloned.1.call-done, s32[4096]{0:T(1024)S(1)} %get-tuple-element.57), kind=kCustom, calls=%fused_computation.4 | custom fusion | bytes 4210688 | tf_op jit(solution)/shard_map/gather | solution.py:41
  281.6 14.9 %gather_fusion.1 = bf16[4096,256]{1,0:T(8,128)(2,1)S(1)} fusion(bf16[4096,256]{1,0:T(8,128)(2,1)} %all-gather.10.cloned.1.call-done, s32[4096]{0:T(1024)S(1)} %get-tuple-element.57), kind=kCustom, calls=%fused_computation.1 | custom fusion | bytes 4210688 | tf_op jit(solution)/shard_map/gather | solution.py:41
  296.5 9.0 %all-gather.18.cloned.1.call-done = bf16[4096,256]{1,0:T(8,128)(2,1)} async-done(((bf16[1024,256]{1,0:T(8,128)(2,1)}), bf16[4096,256]{1,0:T(8,128)(2,1)}) %all-gather.18.cloned.1.call-update) | async-done | bytes 2097168 | tf_op jit(solution)/shard_map/all_gather | solution.py:114
  305.4 17.7 %gather_fusion.8 = bf16[4096,256]{1,0:T(8,128)(2,1)} fusion(bf16[4096,256]{1,0:T(8,128)(2,1)} %all-gather.18.cloned.1.call-done, s32[4096]{0:T(1024)S(1)} %get-tuple-element.57), kind=kCustom, calls=%fused_computation.8 | custom fusion | bytes 4210688 | tf_op jit(solution)/shard_map/gather | solution.py:41
  323.1 10.9 %all-gather.24.cloned.1.call-done = bf16[4096,256]{1,0:T(8,128)(2,1)} async-done(((bf16[512,256]{1,0:T(8,128)(2,1)}), bf16[4096,256]{1,0:T(8,128)(2,1)}) %all-gather.24.cloned.1.call-update) | async-done | bytes 2097168 | tf_op jit(solution)/shard_map/all_gather | solution.py:117
  334.1 17.7 %gather_fusion.11 = bf16[4096,256]{1,0:T(8,128)(2,1)} fusion(bf16[4096,256]{1,0:T(8,128)(2,1)} %all-gather.24.cloned.1.call-done, s32[4096]{0:T(1024)S(1)} %get-tuple-element.56), kind=kCustom, calls=%fused_computation.11 | custom fusion | bytes 4210688 | tf_op jit(solution)/shard_map/gather | solution.py:41
  351.8 12.1 %all-gather.22.cloned.1.call-done = bf16[4096,256]{1,0:T(8,128)(2,1)} async-done(((bf16[512,256]{1,0:T(8,128)(2,1)}), bf16[4096,256]{1,0:T(8,128)(2,1)}) %all-gather.22.cloned.1.call-update) | async-done | bytes 2097168 | tf_op jit(solution)/shard_map/all_gather | solution.py:117
  363.9 17.7 %gather_fusion.10 = bf16[4096,256]{1,0:T(8,128)(2,1)} fusion(bf16[4096,256]{1,0:T(8,128)(2,1)} %all-gather.22.cloned.1.call-done, s32[4096]{0:T(1024)S(1)} %get-tuple-element.56), kind=kCustom, calls=%fused_computation.10 | custom fusion | bytes 4210688 | tf_op jit(solution)/shard_map/gather | solution.py:41
  381.6 12.0 %all-gather.20.cloned.1.call-done = bf16[4096,256]{1,0:T(8,128)(2,1)} async-done(((bf16[512,256]{1,0:T(8,128)(2,1)}), bf16[4096,256]{1,0:T(8,128)(2,1)}) %all-gather.20.cloned.1.call-update) | async-done | bytes 2097168 | tf_op jit(solution)/shard_map/all_gather | solution.py:117
  393.6 17.7 %gather_fusion.9 = bf16[4096,256]{1,0:T(8,128)(2,1)} fusion(bf16[4096,256]{1,0:T(8,128)(2,1)} %all-gather.20.cloned.1.call-done, s32[4096]{0:T(1024)S(1)} %get-tuple-element.56), kind=kCustom, calls=%fused_computation.9 | custom fusion | bytes 4210688 | tf_op jit(solution)/shard_map/gather | solution.py:41
  411.3 1.6 copy-done.1
  412.9 1.9 copy-done.2
  414.8 1.6 copy-done.3
  416.4 1.6 copy-done.4
  417.9 1.6 copy-done.5
  419.6 1.6 copy-done.6
  421.2 44.9 %shard_map.77.refs_2_ = bf16[4096,4096]{1,0:T(8,128)(2,1)} custom-call(bf16[4096,256]{1,0:T(8,128)(2,1)S(1)} %copy-done.2, bf16[4096,256]{1,0:T(8,128)(2,1)S(1)} %copy-done.1, bf16[4096,256]{1,0:T(8,128)(2,1)S(1)} %copy-done.3, bf16[4096,256]{1,0:T(8,128)(2,1)S(1)} %copy-done.6, bf16[4096,256]{1,0:T(8,128)(2,1)S(1)} %copy-done.5, ...), custom_call_target="tpu_custom_call" | custom-call | flops 25769803776 | bytes 67108864 | tf_op jit(solution)/shard_map/pallas_call | solution.py:64
  466.1 17.7 %gather_fusion.2 = bf16[4096,256]{1,0:T(8,128)(2,1)} fusion(bf16[4096,256]{1,0:T(8,128)(2,1)} %all-gather.12.cloned.1.call-done, s32[4096]{0:T(1024)S(1)} %get-tuple-element.56), kind=kCustom, calls=%fused_computation.2 | custom fusion | bytes 4210688 | tf_op jit(solution)/shard_map/gather | solution.py:41
  483.8 1.6 copy-done
  485.4 40.2 %shard_map.78 = bf16[4096,4096]{1,0:T(8,128)(2,1)} custom-call(bf16[4096,256]{1,0:T(8,128)(2,1)S(1)} %gather_fusion.1, bf16[4096,256]{1,0:T(8,128)(2,1)S(1)} %copy-done, bf16[4096,4096]{1,0:T(8,128)(2,1)} %shard_map.77.refs_2_), custom_call_target="tpu_custom_call", output_to_operand_aliasing={{}: (2, {})} | custom-call | flops 8589934592 | bytes 67108864 | tf_op jit(solution)/shard_map/pallas_call | solution.py:64
  (60 shorter events, 5.6 us)
Async XLA Ops:
  13.4 2.2 copy-start.11
  19.1 5.1 copy-start.8
  21.5 2.7 copy-start.9
  30.3 76.6 %all-to-all-start.3 = ((bf16[8,128,256]{2,1,0:T(8,128)(2,1)}), bf16[8,128,256]{2,1,0:T(8,128)(2,1)S(1)}, u32[]{:S(2)}, u32[]{:S(2)}) async-start(bf16[8,128,256]{2,1,0:T(8,128)(2,1)} %bitcast.23), calls=%async_computation.3 | async-start | bytes 1048576 | tf_op jit(solution)/shard_map/all_to_all | solution.py:113
  35.5 209.6 %sort.33.cloned.1.call-start = ((), (), s32[]{:S(2)}) async-start(), calls=%async_computation.16 | async-start | bytes 196640 | tf_op jit(solution)/shard_map/sort | solution.py:96
  106.9 139.2 %all-gather.16.cloned.1.call-start = ((), (), s32[]{:S(2)}) async-start(), calls=%async_computation.11 | async-start | bytes 2621440 | tf_op jit(solution)/shard_map/all_gather | solution.py:114
  106.9 0.8 copy-start.7
  107.7 156.0 %all-gather.14.cloned.1.call-start = ((), (), s32[]{:S(2)}) async-start(), calls=%async_computation.10 | async-start | bytes 2621440 | tf_op jit(solution)/shard_map/all_gather | solution.py:114
  125.8 155.8 %all-gather.10.cloned.1.call-start = ((), (), s32[]{:S(2)}) async-start(), calls=%async_computation.8 | async-start | bytes 2621440 | tf_op jit(solution)/shard_map/all_gather | solution.py:114
  138.4 16.9 %copy-start.10 = (bf16[1024,128]{0,1:T(8,128)(2,1)S(1)}, bf16[1024,128]{0,1:T(8,128)(2,1)}, u32[]{:S(2)}) copy-start(bf16[1024,128]{0,1:T(8,128)(2,1)} %get-tuple-element.51) | copy-start | bytes 786436
  155.2 150.2 %all-gather.18.cloned.1.call-start = ((), (), s32[]{:S(2)}) async-start(), calls=%async_computation.12 | async-start | bytes 2621440 | tf_op jit(solution)/shard_map/all_gather | solution.py:114
  172.4 161.7 %all-gather.24.cloned.1.call-start = ((), (), s32[]{:S(2)}) async-start(), calls=%async_computation.15 | async-start | bytes 2359296 | tf_op jit(solution)/shard_map/all_gather | solution.py:117
  192.3 171.6 %all-gather.22.cloned.1.call-start = ((), (), s32[]{:S(2)}) async-start(), calls=%async_computation.14 | async-start | bytes 2359296 | tf_op jit(solution)/shard_map/all_gather | solution.py:117
  207.8 185.8 %all-gather.20.cloned.1.call-start = ((), (), s32[]{:S(2)}) async-start(), calls=%async_computation.13 | async-start | bytes 2359296 | tf_op jit(solution)/shard_map/all_gather | solution.py:117
  220.0 246.2 %all-gather.12.cloned.1.call-start = ((), (), s32[]{:S(2)}) async-start(), calls=%async_computation.9 | async-start | bytes 2359296 | tf_op jit(solution)/shard_map/all_gather | solution.py:117
  411.3 1.6 copy-start.1
  412.9 1.9 copy-start.2
  414.8 1.6 copy-start.3
  416.4 1.6 copy-start.4
  417.9 1.6 copy-start.5
  419.6 1.6 copy-start.6
  483.8 1.6 copy-start
Sparse Core Ops, SparseCore 0:
  107.0 9.3 sort.35.cloned.1.call-done
  (1 shorter events, 0.0 us)
Sparse Core Ops, SparseCore 1:
  108.9 42.0 all-gather.15
  152.4 55.3 all-gather.13
  209.1 50.1 all-gather.9
  261.0 44.4 all-gather.17
  307.5 26.5 all-gather.23
  336.1 27.7 all-gather.21
  365.8 27.7 all-gather.19
  395.5 27.7 all-gather.11

commit v2 on v0

--- a/solution.py
+++ b/solution.py
@@ -2,11 +2,6 @@
 import jax.numpy as jnp
 from jax import lax
 from jax.sharding import PartitionSpec as P
-
-
-def broadcast(block, axis, source):
-    block = jnp.where(lax.axis_index(axis) == source, block, jnp.zeros_like(block))
-    return lax.psum(block, axis)
 
 
 def apply_mask(panel_block, block_mask, block_width):
@@ -42,31 +37,60 @@
     return jnp.concatenate(solved, axis=1)
 
 
-def arrange(values, positions, base_pos):
-    return values[jnp.argsort(positions - base_pos)]
+def swap(value, axis, distance):
+    count = lax.axis_size(axis)
+    return lax.ppermute(value, axis, [(i, i ^ distance) for i in range(count)])
+
+
+def exchange(groups, axis):
+    count, me = lax.axis_size(axis), lax.axis_index(axis)
+    parts = []
+    for distance in range(count):
+        part = lax.dynamic_index_in_dim(groups, me ^ distance, 0, keepdims=False)
+        parts.append(swap(part, axis, distance) if distance else part)
+    return jnp.concatenate(parts, axis=0)
+
+
+def spread_row(value):
+    count = lax.axis_size("row")
+    held = [value] + [swap(value, "row", distance) for distance in range(2, count, 2)]
+    held = jnp.concatenate(held, axis=0)
+    return jnp.concatenate([held, swap(held, "row", 1)], axis=0)
+
+
+def gather_col(value):
+    count, me = lax.axis_size("col"), lax.axis_index("col")
+    held = [value] + [swap(value, "col", distance) for distance in range(1, count)]
+    stacked = jnp.stack(held)
+    return stacked[me ^ jnp.arange(count)].reshape(-1)
+
+
+def take_rows(values, order):
+    return values.at[order].get(mode="promise_in_bounds", unique_indices=True)
 
 
 def local(panel_block, block_mask, grid_pos, lower_blocks, diag_inv, trailing):
     block_width = diag_inv.shape[1]
+    rows_dev = panel_block.shape[0]
+    n_row, n_col = lax.axis_size("row"), lax.axis_size("col")
+    slot = rows_dev // n_row
+    sorted_pos, by_grid = lax.sort(
+        (grid_pos, lax.iota(jnp.int32, rows_dev)), num_keys=1, is_stable=False
+    )
+    grouped_pos = sorted_pos.reshape(n_row, slot)
+    arrived_pos = lax.all_to_all(grouped_pos, "row", split_axis=0, concat_axis=0, tiled=True)
+    order_row = jnp.argsort(gather_col(arrived_pos.reshape(-1)))
+    order_col = jnp.argsort(spread_row(exchange(grouped_pos[:n_col], "col")))
+
     masked = apply_mask(panel_block, block_mask, block_width)
     factor = solve_panel(masked, lower_blocks, diag_inv)
     columns = factor.shape[1]
-    grid_rows = trailing.shape[0]
-    row_count = lax.axis_size("row")
-    per_row = panel_block.shape[0] // row_count
-    by_grid = jnp.argsort(grid_pos)
-    grouped = factor[by_grid].reshape(row_count, per_row, columns)
-    grouped_pos = grid_pos[by_grid].reshape(row_count, per_row)
-    arrived, arrived_pos = (
-        lax.all_to_all(grouped, "row", split_axis=0, concat_axis=0, tiled=True),
-        lax.all_to_all(grouped_pos, "row", split_axis=0, concat_axis=0, tiled=True),
-    )
-    gathered, gathered_pos = (
-        lax.all_gather(arrived.reshape(-1, columns), "col", axis=0, tiled=True),
-        lax.all_gather(arrived_pos.reshape(-1), "col", axis=0, tiled=True),
-    )
-    row_part = arrange(gathered, gathered_pos, lax.axis_index("row") * grid_rows)
-    column_part = broadcast(row_part, "row", lax.axis_index("col"))
+    grouped = take_rows(factor, by_grid).reshape(n_row, slot, columns)
+    across = exchange(grouped[:n_col], "col")
+    arrived = lax.all_to_all(grouped, "row", split_axis=0, concat_axis=0, tiled=True)
+    gathered = lax.all_gather(arrived.reshape(-1, columns), "col", axis=0, tiled=True)
+    column_part = take_rows(spread_row(across), order_col)
+    row_part = take_rows(gathered, order_row)
     product = lax.dot_general(
         row_part, column_part, (((1,), (1,)), ((), ())), preferred_element_type=jnp.float32
     )

time: 434 us -> 331 us (0.76)
  waiting for transfers between devices: 236 us -> 100 us
  local copies, waits for them, and re-layouts: 43.4 us -> 75.9 us
  starting transfers between devices: 3.39 us -> 24.4 us
  blocking collectives: 51.5 us -> 31.9 us
    psum x1 -> x0, waiting for transfers between devices: 124 us -> none  [broadcast(): return lax.psum(block, axis)]
    all_gather x1, waiting for transfers between devices: 107 us -> 0.01 us  [local(): lax.all_gather(arrived.reshape(-1, columns), 'col', axis=0, tiled=True)]
    ppermute x0 -> x17, waiting for transfers between devices: none -> 100 us  [swap(): return lax.ppermute(value, axis, [(i, i ^ distance) for i in range(count)])]
    ppermute x0 -> x17, starting transfers between devices: none -> 20.9 us  [swap(): return lax.ppermute(value, axis, [(i, i ^ distance) for i in range(count)])]
    all_gather x1 -> x0, blocking collectives: 19.6 us -> none  [local(): lax.all_gather(arrived_pos.reshape(-1), 'col', axis=0, tiled=True)]
    gather x3 -> x4, local copies, waits for them, and re-layouts: 39.5 us -> 56.6 us  [the longest x3 56 us: take_rows(): return values.at[order].get(mode='promise_in_bounds', unique_indices=True)]
    unnamed x7 -> x22, local copies, waits for them, and re-layouts: 3.53 us -> 11.8 us
    select_n x1, other arithmetic: 7.32 us -> 0.01 us  [gather_col(): return stacked[me ^ jnp.arange(count)].reshape(-1)]
  transfers between devices with their start and end apart: 3 -> 19, of which waited for: 3 -> 10; matrix products, arithmetic and copies ran while one was open for 3% -> 16% of each run, Pallas kernels for 0% -> 0%
where the time goes in v2:
time: 331 us; the launch traced here: 330 us
  waiting for transfers between devices  100 us (30%)
  local copies, waits for them, and re-layouts  75.9 us (23%)
  matrix products  64.1 us (19%)
  blocking collectives  31.9 us (10%)
  starting transfers between devices  24.4 us (7%)
  other arithmetic  19.5 us (6%)
  between operations  14.3 us (4%)
    ppermute x17, waiting for transfers between devices, swap(): return lax.ppermute(value, axis, [(i, i ^ distance) for i in range(count)])  100 us
    gather x3, local copies, waits for them, and re-layouts, take_rows(): return values.at[order].get(mode='promise_in_bounds', unique_indices=True)  56 us
    dot_general x1, matrix products, local(): lax.dot_general(row_part, column_part, (((1,), (1,)), ((), ())), preferre...  44.1 us
    all_to_all x1, blocking collectives, local(): lax.all_to_all(grouped, 'row', split_axis=0, concat_axis=0, tiled=True)  31.9 us
    ppermute x17, starting transfers between devices, swap(): return lax.ppermute(value, axis, [(i, i ^ distance) for i in range(count)])  20.9 us
    dot_general x8, matrix products, solve_panel(): lax.dot_general(residue, diag_inv[block_index], (((1,), (1,)), ((), ())),...  20 us
    unnamed x22, local copies, waits for them, and re-layouts  11.8 us
  transfers between devices with their start and end apart: 19, of which 10 were waited for; matrix products, arithmetic and copies ran while one was open for 16% of the time, Pallas kernels for 0%

profile of v2, /device:TPU:0, one launch (start us, length us, event | category | flops | bytes accessed | tf_op | source)
XLA Modules:
  0.0 330.1 jit_solution(17271777549402978106)
XLA Ops:
  7.9 4.9 %sort.46 = (s32[1024]{0:T(1024)}, s32[1024]{0:T(1024)S(1)}) sort(s32[1024]{0:T(1024)} %param.8, s32[1024]{0:T(1024)S(1)} %iota.14), dimensions={0}, to_apply=%region_0.0 | sort | flops 10240 | bytes 16384 | tf_op jit(solution)/shard_map/sort | solution.py:77
  13.2 2.2 bitcast_select_fusion
  15.4 1.3 constant_dynamic-update-slice_fusion.17
  16.6 2.2 constant_dynamic-update-slice_fusion.16
  18.9 2.4 constant_dynamic-update-slice_fusion.15
  21.3 2.5 constant_dynamic-update-slice_fusion.14
  23.8 2.6 constant_dynamic-update-slice_fusion.13
  26.3 2.9 constant_dynamic-update-slice_fusion.12
  29.3 3.0 constant_dynamic-update-slice_fusion.11
  32.3 3.1 fusion.6
  35.4 2.9 copy.11
  38.2 5.3 %gather_fusion = bf16[1024,1024]{1,0:T(8,128)(2,1)} fusion(bf16[1024,1024]{1,0:T(8,128)(2,1)S(1)} %copy.11, s32[1024]{0:T(1024)S(1)} %fusion.85), kind=kCustom, calls=%fused_computation | custom fusion | bytes 4198400 | tf_op jit(solution)/shard_map/gather | solution.py:69
  43.6 31.9 %all_to_all.14 = bf16[8,128,1024]{2,1,0:T(8,128)(2,1)} all-to-all(bf16[8,128,1024]{2,1,0:T(8,128)(2,1)} %bitcast.83), channel_id=1, replica_groups=mesh['row'=8,'col'=4] {'row'}, dimensions={0} | all-to-all | bytes 4194304 | tf_op jit(solution)/shard_map/all_to_all | solution.py:90
  75.5 1.5 copy-done.1
  77.2 4.2 %collective-permute-start.5 = (bf16[128,1024]{1,0:T(8,128)(2,1)S(1)}, bf16[128,1024]{1,0:T(8,128)(2,1)S(1)}, u32[]{:S(2)}, u32[]{:S(2)}) collective-permute-start(bf16[128,1024]{1,0:T(8,128)(2,1)S(1)} %get-tuple-element.24), channel_id=1, source_target_pairs={{0,3},{1,2},{2,1},{3,0},{4,7},{5,6},{6,5},{7,4},{8,11},{9,10},{10,... | collective-permute-start | bytes 786440 | tf_op jit(solution)/shard_map/ppermute | solution.py:42
  82.0 0.8 constant_dynamic-update-slice_fusion.31
  82.8 8.0 %collective-permute-done.5 = bf16[128,1024]{1,0:T(8,128)(2,1)S(1)} collective-permute-done((bf16[128,1024]{1,0:T(8,128)(2,1)S(1)}, bf16[128,1024]{1,0:T(8,128)(2,1)S(1)}, u32[]{:S(2)}, u32[]{:S(2)}) %collective-permute-start.5) | collective-permute-done | bytes 262176 | tf_op jit(solution)/shard_map/ppermute | solution.py:42
  90.8 40.5 %collective-permute-done.4 = bf16[128,1024]{1,0:T(8,128)(2,1)S(1)} collective-permute-done((bf16[128,1024]{1,0:T(8,128)(2,1)S(1)}, bf16[128,1024]{1,0:T(8,128)(2,1)S(1)}, u32[]{:S(2)}, u32[]{:S(2)}) %collective-permute-start.4) | collective-permute-done | bytes 262176 | tf_op jit(solution)/shard_map/ppermute | solution.py:42
  131.3 1.3 collective-permute-start.6
  133.1 1.8 collective-permute-start.8
  134.9 0.7 constant_dynamic-update-slice_fusion.39
  135.6 0.8 constant_dynamic-update-slice_fusion.30
  136.5 0.8 constant_dynamic-update-slice_fusion.29
  137.3 0.8 constant_dynamic-update-slice_fusion.28
  138.2 19.3 %collective-permute-done.6 = bf16[512,1024]{1,0:T(8,128)(2,1)S(1)} collective-permute-done((bf16[512,1024]{1,0:T(8,128)(2,1)S(1)}, bf16[512,1024]{1,0:T(8,128)(2,1)S(1)}, u32[]{:S(2)}, u32[]{:S(2)}) %collective-permute-start.6) | collective-permute-done | bytes 1048608 | tf_op jit(solution)/shard_map/ppermute | solution.py:42
  157.5 1.7 constant_dynamic-update-slice_fusion.27
  159.2 18.0 %collective-permute-done.7 = bf16[512,1024]{1,0:T(8,128)(2,1)S(1)} collective-permute-done((bf16[512,1024]{1,0:T(8,128)(2,1)S(1)}, bf16[512,1024]{1,0:T(8,128)(2,1)S(1)}, u32[]{:S(2)}, u32[]{:S(2)}) %collective-permute-start.7) | collective-permute-done | bytes 1048608 | tf_op jit(solution)/shard_map/ppermute | solution.py:42
  177.2 1.7 constant_dynamic-update-slice_fusion.26
  178.9 1.7 constant_dynamic-update-slice_fusion.25
  180.6 3.5 %all-to-all-start.1 = ((s32[8,1,128]{2,1,0:T(1,128)}), s32[8,1,128]{2,1,0:T(1,128)S(1)}, u32[]{:S(2)}, u32[]{:S(2)}) async-start(s32[8,1,128]{2,1,0:T(1,128)} %bitcast.10), calls=%async_computation.1 | async-start | bytes 8192 | tf_op jit(solution)/shard_map/all_to_all | solution.py:81
  184.9 4.3 %collective-permute-start.10 = (s32[128]{0:T(128)S(1)}, s32[128]{0:T(128)S(1)}, u32[]{:S(2)}, u32[]{:S(2)}) collective-permute-start(s32[128]{0:T(128)S(1)} %get-tuple-element.66), channel_id=1, source_target_pairs={{0,1},{1,0},{2,3},{3,2},{4,5},{5,4},{6,7},{7,6},{8,9},{9,8},{10,11... | collective-permute-start | bytes 1544 | tf_op jit(solution)/shard_map/ppermute | solution.py:42
  189.3 1.0 collective-permute-done.12
  190.3 4.0 %collective-permute-done.11 = s32[128]{0:T(128)S(1)} collective-permute-done((s32[128]{0:T(128)S(1)}, s32[128]{0:T(128)S(1)}, u32[]{:S(2)}, u32[]{:S(2)}) %collective-permute-start.11) | collective-permute-done | bytes 544 | tf_op jit(solution)/shard_map/ppermute | solution.py:42
  194.3 1.2 collective-permute-start.15
  195.5 1.6 collective-permute-start.14
  197.1 0.7 collective-permute-start.13
  197.9 2.8 collective-permute-done.13
  200.7 3.6 %collective-permute-start.2 = (s32[1024]{0:T(1024)S(1)}, s32[1024]{0:T(1024)S(1)}, u32[]{:S(2)}, u32[]{:S(2)}) collective-permute-start(s32[1024]{0:T(1024)S(1)} %bitcast.90), channel_id=1, source_target_pairs={{0,3},{1,2},{2,1},{3,0},{4,7},{5,6},{6,5},{7,4},{8,11},{9,10},{10,... | collective-permute-start | bytes 12296 | tf_op jit(solution)/shard_map/ppermute | solution.py:42
  204.3 0.9 collective-permute-start
  205.3 1.1 collective-permute-done.2
  206.4 2.5 collective-permute-done.1
  208.9 2.7 collective-permute-done
  212.3 5.8 %sort.47 = (s32[4096]{0:T(1024)}, s32[4096]{0:T(1024)S(1)}) sort(s32[4096]{0:T(1024)S(1)} %bitcast.89, s32[4096]{0:T(1024)S(1)} %iota.16), dimensions={0}, to_apply=%region_1.0 | sort | flops 49152 | bytes 65536 | tf_op jit(solution)/shard_map/jit(argsort)/sort | solution.py:82
  218.0 5.8 %sort.48 = (s32[4096]{0:T(1024)}, s32[4096]{0:T(1024)S(1)}) sort(s32[4096]{0:T(1024)S(1)} %constant_dynamic-update-slice_fusion.54, s32[4096]{0:T(1024)S(1)} %iota.17), dimensions={0}, to_apply=%region_2.3 | sort | flops 49152 | bytes 65536 | tf_op jit(solution)/shard_map/jit(argsort)/sort | solution.py:83
  223.8 4.6 %constant_dynamic-update-slice_fusion.32 = bf16[4096,1024]{1,0:T(8,128)(2,1)} fusion(bf16[4096,1024]{1,0:T(8,128)(2,1)} %get-tuple-element.19, bf16[2048,1024]{1,0:T(8,128)(2,1)} %collective-permute-done.9), kind=kLoop, calls=%fused_computation.101 | loop fusion | bytes 8388608 | tf_op jit(solution)/shard_map/concatenate | solution.py:58
  228.5 25.3 %gather_fusion.3 = bf16[4096,1024]{1,0:T(8,128)(2,1)} fusion(bf16[4096,1024]{1,0:T(8,128)(2,1)} %constant_dynamic-update-slice_fusion.32, s32[4096]{0:T(1024)S(1)} %get-tuple-element.78), kind=kCustom, calls=%fused_computation.3 | custom fusion | bytes 16793600 | tf_op jit(solution)/shard_map/gather | solution.py:69
  253.8 25.3 %gather_fusion.2 = bf16[4096,1024]{1,0:T(8,128)(2,1)} fusion(bf16[4096,1024]{1,0:T(8,128)(2,1)} %all-gather.2.cloned.1.call-done, s32[4096]{0:T(1024)S(1)} %get-tuple-element.77), kind=kCustom, calls=%fused_computation.2 | custom fusion | bytes 16793600 | tf_op jit(solution)/shard_map/gather | solution.py:69
  279.1 44.1 %subtract_convert_fusion = bf16[4096,4096]{1,0:T(8,128)(2,1)} fusion(bf16[4096,4096]{1,0:T(8,128)(2,1)} %param.11, bf16[4096,1024]{1,0:T(8,128)(2,1)} %gather_fusion.2, bf16[4096,1024]{1,0:T(8,128)(2,1)} %gather_fusion.3), kind=kOutput, calls=%fused_computation.4 | convolution fusion | flops 34410070016 | bytes 83886080 | tf_op jit(solution)/shard_map/dot_general | solution.py:94
  (53 shorter events, 4.0 us)
Async XLA Ops:
  7.2 246.6 %all-gather.2.cloned.1.call-start = ((), (), s32[]{:S(2)}) async-start(), calls=%async_computation.2 | async-start | bytes 10485760 | tf_op jit(solution)/shard_map/all_gather | solution.py:91
  13.2 2.2 copy-start.2
  38.2 5.4 %copy-start = (bf16[1024,1024]{1,0:T(8,128)(2,1)}, bf16[1024,1024]{1,0:T(8,128)(2,1)S(1)}, u32[]{:S(2)}) copy-start(bf16[1024,1024]{1,0:T(8,128)(2,1)S(1)} %copy.11) | copy-start | bytes 6291460
  75.5 1.6 copy-start.1
  77.2 13.6 %collective-permute-start.5 = (bf16[128,1024]{1,0:T(8,128)(2,1)S(1)}, bf16[128,1024]{1,0:T(8,128)(2,1)S(1)}, u32[]{:S(2)}, u32[]{:S(2)}) collective-permute-start(bf16[128,1024]{1,0:T(8,128)(2,1)S(1)} %get-tuple-element.24), channel_id=1, source_target_pairs={{0,3},{1,2},{2,1},{3,0},{4,7},{5,6},{6,5},{7,4},{8,11},{9,10},{10,... | collective-permute-start | bytes 786440 | tf_op jit(solution)/shard_map/ppermute | solution.py:42
  81.4 49.9 %collective-permute-start.4 = (bf16[128,1024]{1,0:T(8,128)(2,1)S(1)}, bf16[128,1024]{1,0:T(8,128)(2,1)S(1)}, u32[]{:S(2)}, u32[]{:S(2)}) collective-permute-start(bf16[128,1024]{1,0:T(8,128)(2,1)S(1)} %get-tuple-element.25), channel_id=1, source_target_pairs={{0,2},{1,3},{2,0},{3,1},{4,6},{5,7},{6,4},{7,5},{8,10},{9,11},{10,... | collective-permute-start | bytes 786440 | tf_op jit(solution)/shard_map/ppermute | solution.py:42
  81.4 49.9 %collective-permute-start.3 = (bf16[128,1024]{1,0:T(8,128)(2,1)S(1)}, bf16[128,1024]{1,0:T(8,128)(2,1)S(1)}, u32[]{:S(2)}, u32[]{:S(2)}) collective-permute-start(bf16[128,1024]{1,0:T(8,128)(2,1)S(1)} %get-tuple-element.26), channel_id=1, source_target_pairs={{0,1},{1,0},{2,3},{3,2},{4,5},{5,4},{6,7},{7,6},{8,9},{9,8},{10,11... | collective-permute-start | bytes 786440 | tf_op jit(solution)/shard_map/ppermute | solution.py:42
  131.3 26.2 %collective-permute-start.6 = (bf16[512,1024]{1,0:T(8,128)(2,1)S(1)}, bf16[512,1024]{1,0:T(8,128)(2,1)S(1)}, u32[]{:S(2)}, u32[]{:S(2)}) collective-permute-start(bf16[512,1024]{1,0:T(8,128)(2,1)S(1)} %pad_maximum_fusion), channel_id=1, source_target_pairs={{0,8},{4,12},{8,0},{12,4},{16,24},{20,28},{24,16},{28,20},{1,9},{5... | collective-permute-start | bytes 3145736 | tf_op jit(solution)/shard_map/ppermute | solution.py:42
  132.7 44.5 %collective-permute-start.7 = (bf16[512,1024]{1,0:T(8,128)(2,1)S(1)}, bf16[512,1024]{1,0:T(8,128)(2,1)S(1)}, u32[]{:S(2)}, u32[]{:S(2)}) collective-permute-start(bf16[512,1024]{1,0:T(8,128)(2,1)S(1)} %pad_maximum_fusion), channel_id=1, source_target_pairs={{0,16},{4,20},{8,24},{12,28},{16,0},{20,4},{24,8},{28,12},{1,17},{... | collective-permute-start | bytes 3145736 | tf_op jit(solution)/shard_map/ppermute | solution.py:42
  133.1 45.8 %collective-permute-start.8 = (bf16[512,1024]{1,0:T(8,128)(2,1)S(1)}, bf16[512,1024]{1,0:T(8,128)(2,1)S(1)}, u32[]{:S(2)}, u32[]{:S(2)}) collective-permute-start(bf16[512,1024]{1,0:T(8,128)(2,1)S(1)} %pad_maximum_fusion), channel_id=1, source_target_pairs={{0,24},{4,28},{8,16},{12,20},{16,8},{20,12},{24,0},{28,4},{1,25},{... | collective-permute-start | bytes 3145736 | tf_op jit(solution)/shard_map/ppermute | solution.py:42
  180.6 43.3 %collective-permute-start.9 = (bf16[2048,1024]{1,0:T(8,128)(2,1)}, bf16[2048,1024]{1,0:T(8,128)(2,1)}, u32[]{:S(2)}, u32[]{:S(2)}) collective-permute-start(bf16[2048,1024]{1,0:T(8,128)(2,1)} %get-tuple-element.18), channel_id=1, source_target_pairs={{0,4},{4,0},{8,12},{12,8},{16,20},{20,16},{24,28},{28,24},{1,5},{5... | collective-permute-start | bytes 12582920 | tf_op jit(solution)/shard_map/ppermute | solution.py:42
  180.6 20.2 %all-to-all-start.1 = ((s32[8,1,128]{2,1,0:T(1,128)}), s32[8,1,128]{2,1,0:T(1,128)S(1)}, u32[]{:S(2)}, u32[]{:S(2)}) async-start(s32[8,1,128]{2,1,0:T(1,128)} %bitcast.10), calls=%async_computation.1 | async-start | bytes 8192 | tf_op jit(solution)/shard_map/all_to_all | solution.py:81
  184.8 5.5 %collective-permute-start.12 = (s32[128]{0:T(128)S(1)}, s32[128]{0:T(128)S(1)}, u32[]{:S(2)}, u32[]{:S(2)}) collective-permute-start(s32[128]{0:T(128)S(1)} %get-tuple-element.64), channel_id=1, source_target_pairs={{0,3},{1,2},{2,1},{3,0},{4,7},{5,6},{6,5},{7,4},{8,11},{9,10},{10,... | collective-permute-start | bytes 1544 | tf_op jit(solution)/shard_map/ppermute | solution.py:42
  184.9 9.4 %collective-permute-start.11 = (s32[128]{0:T(128)S(1)}, s32[128]{0:T(128)S(1)}, u32[]{:S(2)}, u32[]{:S(2)}) collective-permute-start(s32[128]{0:T(128)S(1)} %get-tuple-element.65), channel_id=1, source_target_pairs={{0,2},{1,3},{2,0},{3,1},{4,6},{5,7},{6,4},{7,5},{8,10},{9,11},{10,... | collective-permute-start | bytes 1544 | tf_op jit(solution)/shard_map/ppermute | solution.py:42
  184.9 9.3 %collective-permute-start.10 = (s32[128]{0:T(128)S(1)}, s32[128]{0:T(128)S(1)}, u32[]{:S(2)}, u32[]{:S(2)}) collective-permute-start(s32[128]{0:T(128)S(1)} %get-tuple-element.66), channel_id=1, source_target_pairs={{0,1},{1,0},{2,3},{3,2},{4,5},{5,4},{6,7},{7,6},{8,9},{9,8},{10,11... | collective-permute-start | bytes 1544 | tf_op jit(solution)/shard_map/ppermute | solution.py:42
  194.3 10.9 %collective-permute-start.15 = (s32[512]{0:T(512)S(1)}, s32[512]{0:T(512)S(1)}, u32[]{:S(2)}, u32[]{:S(2)}) collective-permute-start(s32[512]{0:T(512)S(1)} %pad_add_fusion.1), channel_id=1, source_target_pairs={{0,24},{4,28},{8,16},{12,20},{16,8},{20,12},{24,0},{28,4},{1,25},{... | collective-permute-start | bytes 6152 | tf_op jit(solution)/shard_map/ppermute | solution.py:42
  195.5 5.2 %collective-permute-start.14 = (s32[512]{0:T(512)S(1)}, s32[512]{0:T(512)S(1)}, u32[]{:S(2)}, u32[]{:S(2)}) collective-permute-start(s32[512]{0:T(512)S(1)} %pad_add_fusion.1), channel_id=1, source_target_pairs={{0,16},{4,20},{8,24},{12,28},{16,0},{20,4},{24,8},{28,12},{1,17},{... | collective-permute-start | bytes 6152 | tf_op jit(solution)/shard_map/ppermute | solution.py:42
  197.1 3.6 %collective-permute-start.13 = (s32[512]{0:T(512)S(1)}, s32[512]{0:T(512)S(1)}, u32[]{:S(2)}, u32[]{:S(2)}) collective-permute-start(s32[512]{0:T(512)S(1)} %pad_add_fusion.1), channel_id=1, source_target_pairs={{0,8},{4,12},{8,0},{12,4},{16,24},{20,28},{24,16},{28,20},{1,9},{5... | collective-permute-start | bytes 6152 | tf_op jit(solution)/shard_map/ppermute | solution.py:42
  200.7 5.6 %collective-permute-start.2 = (s32[1024]{0:T(1024)S(1)}, s32[1024]{0:T(1024)S(1)}, u32[]{:S(2)}, u32[]{:S(2)}) collective-permute-start(s32[1024]{0:T(1024)S(1)} %bitcast.90), channel_id=1, source_target_pairs={{0,3},{1,2},{2,1},{3,0},{4,7},{5,6},{6,5},{7,4},{8,11},{9,10},{10,... | collective-permute-start | bytes 12296 | tf_op jit(solution)/shard_map/ppermute | solution.py:42
  204.3 4.6 %collective-permute-start.1 = (s32[1024]{0:T(1024)S(1)}, s32[1024]{0:T(1024)S(1)}, u32[]{:S(2)}, u32[]{:S(2)}) collective-permute-start(s32[1024]{0:T(1024)S(1)} %bitcast.91), channel_id=1, source_target_pairs={{0,2},{1,3},{2,0},{3,1},{4,6},{5,7},{6,4},{7,5},{8,10},{9,11},{10,... | collective-permute-start | bytes 12296 | tf_op jit(solution)/shard_map/ppermute | solution.py:42
  204.3 7.4 %collective-permute-start = (s32[1024]{0:T(1024)S(1)}, s32[1024]{0:T(1024)S(1)}, u32[]{:S(2)}, u32[]{:S(2)}) collective-permute-start(s32[1024]{0:T(1024)S(1)} %bitcast.92), channel_id=1, source_target_pairs={{0,1},{1,0},{2,3},{3,2},{4,5},{5,4},{6,7},{7,6},{8,9},{9,8},{10,11... | collective-permute-start | bytes 12296 | tf_op jit(solution)/shard_map/ppermute | solution.py:42
  205.2 12.8 %collective-permute-start.16 = (s32[2048]{0:T(1024)S(1)}, s32[2048]{0:T(1024)S(1)}, u32[]{:S(2)}, u32[]{:S(2)}) collective-permute-start(s32[2048]{0:T(1024)S(1)} %get-tuple-element.58), channel_id=1, source_target_pairs={{0,4},{4,0},{8,12},{12,8},{16,20},{20,16},{24,28},{28,24},{1,5},{5... | collective-permute-start | bytes 24584 | tf_op jit(solution)/shard_map/ppermute | solution.py:42
Sparse Core Ops, SparseCore 0:
  75.6 163.3 all-gather.1

commit v3 on v2

--- a/solution.py
+++ b/solution.py
@@ -88,6 +88,7 @@
     grouped = take_rows(factor, by_grid).reshape(n_row, slot, columns)
     across = exchange(grouped[:n_col], "col")
     arrived = lax.all_to_all(grouped, "row", split_axis=0, concat_axis=0, tiled=True)
+    arrived, across = lax.optimization_barrier((arrived, across))
     gathered = lax.all_gather(arrived.reshape(-1, columns), "col", axis=0, tiled=True)
     column_part = take_rows(spread_row(across), order_col)
     row_part = take_rows(gathered, order_row)

time: 331 us -> 304 us (0.918)
  blocking collectives: 31.9 us -> 0 us
  starting transfers between devices: 24.4 us -> 31.1 us
  local copies, waits for them, and re-layouts: 75.9 us -> 70.2 us
    all_to_all x1 -> x0, blocking collectives: 31.9 us -> none  [local(): lax.all_to_all(grouped, 'row', split_axis=0, concat_axis=0, tiled=True)]
    all_gather x1, waiting for transfers between devices: 0.01 us -> 21 us  [local(): lax.all_gather(arrived.reshape(-1, columns), 'col', axis=0, tiled=True)]
    ppermute x17, waiting for transfers between devices: 100 us -> 80.6 us  [swap(): return lax.ppermute(value, axis, [(i, i ^ distance) for i in range(count)])]
    all_to_all x0 -> x1, starting transfers between devices: none -> 5.3 us  [local(): lax.all_to_all(grouped, 'row', split_axis=0, concat_axis=0, tiled=True)]
    unnamed x22 -> x23, local copies, waits for them, and re-layouts: 11.8 us -> 7.63 us
  transfers between devices with their start and end apart: 19 -> 20, of which waited for: 10 -> 11; matrix products, arithmetic and copies ran while one was open for 16% -> 16% of each run, Pallas kernels for 0% -> 0%
where the time goes in v3:
time: 304 us; the launch traced here: 303 us
  waiting for transfers between devices  102 us (34%)
  local copies, waits for them, and re-layouts  70.2 us (23%)
  matrix products  64.1 us (21%)
  starting transfers between devices  31.1 us (10%)
  other arithmetic  21.8 us (7%)
  between operations  14.3 us (5%)
    ppermute x17, waiting for transfers between devices, swap(): return lax.ppermute(value, axis, [(i, i ^ distance) for i in range(count)])  80.6 us
    gather x3, local copies, waits for them, and re-layouts, take_rows(): return values.at[order].get(mode='promise_in_bounds', unique_indices=True)  56.1 us
    dot_general x1, matrix products, local(): lax.dot_general(row_part, column_part, (((1,), (1,)), ((), ())), preferre...  44.1 us
    ppermute x17, starting transfers between devices, swap(): return lax.ppermute(value, axis, [(i, i ^ distance) for i in range(count)])  22.3 us
    all_gather x1, waiting for transfers between devices, local(): lax.all_gather(arrived.reshape(-1, columns), 'col', axis=0, tiled=True)  21 us
    dot_general x8, matrix products, solve_panel(): lax.dot_general(residue, diag_inv[block_index], (((1,), (1,)), ((), ())),...  20 us
    unnamed x23, local copies, waits for them, and re-layouts  7.63 us
  transfers between devices with their start and end apart: 20, of which 11 were waited for; matrix products, arithmetic and copies ran while one was open for 16% of the time, Pallas kernels for 0%

profile of v3, /device:TPU:0, one launch (start us, length us, event | category | flops | bytes accessed | tf_op | source)
XLA Modules:
  0.0 303.0 jit_solution(917924162712501019)
XLA Ops:
  7.2 0.7 broadcast_compare_fusion
  7.9 4.9 %sort.46 = (s32[1024]{0:T(1024)}, s32[1024]{0:T(1024)S(1)}) sort(s32[1024]{0:T(1024)} %param.8, s32[1024]{0:T(1024)S(1)} %iota.14), dimensions={0}, to_apply=%region_0.0 | sort | flops 10240 | bytes 16384 | tf_op jit(solution)/shard_map/sort | solution.py:77
  13.1 2.2 bitcast_select_fusion
  15.3 1.3 constant_dynamic-update-slice_fusion.17
  16.6 2.2 constant_dynamic-update-slice_fusion.16
  18.8 2.4 constant_dynamic-update-slice_fusion.15
  21.2 2.5 constant_dynamic-update-slice_fusion.14
  23.7 2.6 constant_dynamic-update-slice_fusion.13
  26.3 2.9 constant_dynamic-update-slice_fusion.12
  29.2 3.0 constant_dynamic-update-slice_fusion.11
  32.2 3.1 %fusion.6 = bf16[1024,1024]{0,1:T(8,128)(2,1)} fusion(bf16[1024,1024]{0,1:T(8,128)(2,1)} %get-tuple-element.25, bf16[1024,896]{0,1:T(8,128)(2,1)} %get-tuple-element.24, bf16[1024,1024]{1,0:T(8,128)(2,1)S(1)} %bitcast_select_fusion, bf16[1024,1024]{1,0:T(8,128)(2,1)} %param.9, bf16[8,128,128]{2,1,0:T(8,128)(2,1)S(1)} %copy-done.4), kind=kOutput, calls=%fused_computation.21 | convolution fusion | flops 268959744 | bytes 2621440 | tf_op jit(solution)/shard_map/dot_general | solution.py:30
  35.3 2.9 copy.11
  38.2 5.3 %gather_fusion = bf16[1024,1024]{1,0:T(8,128)(2,1)} fusion(bf16[1024,1024]{1,0:T(8,128)(2,1)S(1)} %copy.11, s32[1024]{0:T(1024)S(1)} %fusion.85), kind=kCustom, calls=%fused_computation | custom fusion | bytes 4198400 | tf_op jit(solution)/shard_map/gather | solution.py:69
  43.5 5.3 %all-to-all-start = ((bf16[8,128,1024]{2,1,0:T(8,128)(2,1)}), bf16[8,128,1024]{2,1,0:T(8,128)(2,1)}, u32[]{:S(2)}, u32[]{:S(2)}) async-start(bf16[8,128,1024]{2,1,0:T(8,128)(2,1)} %bitcast.82), calls=%async_computation | async-start | bytes 4194304 | tf_op jit(solution)/shard_map/all_to_all | solution.py:90
  49.1 4.3 %collective-permute-start.2 = (bf16[128,1024]{1,0:T(8,128)(2,1)S(1)}, bf16[128,1024]{1,0:T(8,128)(2,1)S(1)}, u32[]{:S(2)}, u32[]{:S(2)}) collective-permute-start(bf16[128,1024]{1,0:T(8,128)(2,1)S(1)} %get-tuple-element.21), channel_id=1, source_target_pairs={{0,3},{1,2},{2,1},{3,0},{4,7},{5,6},{6,5},{7,4},{8,11},{9,10},{10,... | collective-permute-start | bytes 786440 | tf_op jit(solution)/shard_map/ppermute | solution.py:42
  53.4 0.6 collective-permute-start
  54.0 6.6 %collective-permute-done.2 = bf16[128,1024]{1,0:T(8,128)(2,1)S(1)} collective-permute-done((bf16[128,1024]{1,0:T(8,128)(2,1)S(1)}, bf16[128,1024]{1,0:T(8,128)(2,1)S(1)}, u32[]{:S(2)}, u32[]{:S(2)}) %collective-permute-start.2) | collective-permute-done | bytes 262176 | tf_op jit(solution)/shard_map/ppermute | solution.py:42
  60.6 15.6 %collective-permute-done.1 = bf16[128,1024]{1,0:T(8,128)(2,1)S(1)} collective-permute-done((bf16[128,1024]{1,0:T(8,128)(2,1)S(1)}, bf16[128,1024]{1,0:T(8,128)(2,1)S(1)}, u32[]{:S(2)}, u32[]{:S(2)}) %collective-permute-start.1) | collective-permute-done | bytes 262176 | tf_op jit(solution)/shard_map/ppermute | solution.py:42
  76.3 2.7 collective-permute-start.8
  79.9 23.5 %collective-permute-done.8 = bf16[512,1024]{1,0:T(8,128)(2,1)S(1)} collective-permute-done((bf16[512,1024]{1,0:T(8,128)(2,1)S(1)}, bf16[512,1024]{1,0:T(8,128)(2,1)S(1)}, u32[]{:S(2)}, u32[]{:S(2)}) %collective-permute-start.8) | collective-permute-done | bytes 1048608 | tf_op jit(solution)/shard_map/ppermute | solution.py:42
  103.4 20.9 %collective-permute-done.7 = bf16[512,1024]{1,0:T(8,128)(2,1)S(1)} collective-permute-done((bf16[512,1024]{1,0:T(8,128)(2,1)S(1)}, bf16[512,1024]{1,0:T(8,128)(2,1)S(1)}, u32[]{:S(2)}, u32[]{:S(2)}) %collective-permute-start.7) | collective-permute-done | bytes 1048608 | tf_op jit(solution)/shard_map/ppermute | solution.py:42
  124.4 2.3 pad_maximum_fusion
  126.8 3.4 %all-to-all-start.1 = ((s32[8,1,128]{2,1,0:T(1,128)}), s32[8,1,128]{2,1,0:T(1,128)S(1)}, u32[]{:S(2)}, u32[]{:S(2)}) async-start(s32[8,1,128]{2,1,0:T(1,128)} %bitcast.15), calls=%async_computation.1 | async-start | bytes 8192 | tf_op jit(solution)/shard_map/all_to_all | solution.py:81
  130.2 0.7 slice_bitcast_fusion
  130.9 2.6 collective-permute-start.12
  133.5 1.8 collective-permute-start.10
  135.4 0.9 collective-permute-done.12
  136.3 3.1 %collective-permute-done.11 = s32[128]{0:T(128)S(1)} collective-permute-done((s32[128]{0:T(128)S(1)}, s32[128]{0:T(128)S(1)}, u32[]{:S(2)}, u32[]{:S(2)}) %collective-permute-start.11) | collective-permute-done | bytes 544 | tf_op jit(solution)/shard_map/ppermute | solution.py:42
  139.5 2.9 collective-permute-start.15
  142.3 1.9 collective-permute-start.14
  144.3 3.5 %collective-permute-done.13 = s32[512]{0:T(512)S(1)} collective-permute-done((s32[512]{0:T(512)S(1)}, s32[512]{0:T(512)S(1)}, u32[]{:S(2)}, u32[]{:S(2)}) %collective-permute-start.13) | collective-permute-done | bytes 2080 | tf_op jit(solution)/shard_map/ppermute | solution.py:42
  147.9 0.7 collective-permute-start.5
  148.6 3.8 %collective-permute-start.3 = (s32[1024]{0:T(1024)S(1)}, s32[1024]{0:T(1024)S(1)}, u32[]{:S(2)}, u32[]{:S(2)}) collective-permute-start(s32[1024]{0:T(1024)S(1)} %bitcast.89), channel_id=1, source_target_pairs={{0,1},{1,0},{2,3},{3,2},{4,5},{5,4},{6,7},{7,6},{8,9},{9,8},{10,11... | collective-permute-start | bytes 12296 | tf_op jit(solution)/shard_map/ppermute | solution.py:42
  152.4 1.1 collective-permute-done.5
  153.5 5.2 %collective-permute-done.3 = s32[1024]{0:T(1024)S(1)} collective-permute-done((s32[1024]{0:T(1024)S(1)}, s32[1024]{0:T(1024)S(1)}, u32[]{:S(2)}, u32[]{:S(2)}) %collective-permute-start.3) | collective-permute-done | bytes 4128 | tf_op jit(solution)/shard_map/ppermute | solution.py:42
  158.8 0.6 gather_fusion.1
  159.3 5.8 %sort.47 = (s32[4096]{0:T(1024)}, s32[4096]{0:T(1024)S(1)}) sort(s32[4096]{0:T(1024)S(1)} %bitcast.86, s32[4096]{0:T(1024)S(1)} %iota.16), dimensions={0}, to_apply=%region_1.0 | sort | flops 49152 | bytes 65536 | tf_op jit(solution)/shard_map/jit(argsort)/sort | solution.py:82
  165.1 5.8 %sort.48 = (s32[4096]{0:T(1024)}, s32[4096]{0:T(1024)S(1)}) sort(s32[4096]{0:T(1024)S(1)} %constant_dynamic-update-slice_fusion.44, s32[4096]{0:T(1024)S(1)} %iota.17), dimensions={0}, to_apply=%region_2.3 | sort | flops 49152 | bytes 65536 | tf_op jit(solution)/shard_map/jit(argsort)/sort | solution.py:83
  170.9 1.0 constant_dynamic-update-slice_fusion.29
  172.0 0.6 copy-done.3
  172.5 1.0 constant_dynamic-update-slice_fusion.28
  173.6 1.0 constant_dynamic-update-slice_fusion.27
  174.6 1.0 constant_dynamic-update-slice_fusion.26
  175.6 4.7 %constant_dynamic-update-slice_fusion.25 = bf16[4096,1024]{1,0:T(8,128)(2,1)} fusion(bf16[4096,1024]{1,0:T(8,128)(2,1)} %constant_dynamic-update-slice_fusion.26, bf16[2048,1024]{1,0:T(8,128)(2,1)} %collective-permute-done.9), kind=kLoop, calls=%fused_computation.95 | loop fusion | bytes 8388608 | tf_op jit(solution)/shard_map/concatenate | solution.py:58
  180.3 25.4 %gather_fusion.3 = bf16[4096,1024]{1,0:T(8,128)(2,1)} fusion(bf16[4096,1024]{1,0:T(8,128)(2,1)} %constant_dynamic-update-slice_fusion.25, s32[4096]{0:T(1024)S(1)} %get-tuple-element.69), kind=kCustom, calls=%fused_computation.3 | custom fusion | bytes 16793600 | tf_op jit(solution)/shard_map/gather | solution.py:69
  205.7 21.0 %all-gather.2.cloned.1.call-done = bf16[4096,1024]{1,0:T(8,128)(2,1)} async-done(((bf16[1024,1024]{1,0:T(8,128)(2,1)}), bf16[4096,1024]{1,0:T(8,128)(2,1)}) %all-gather.2.cloned.1.call-update) | async-done | bytes 8388624 | tf_op jit(solution)/shard_map/all_gather | solution.py:92
  226.7 25.3 %gather_fusion.2 = bf16[4096,1024]{1,0:T(8,128)(2,1)} fusion(bf16[4096,1024]{1,0:T(8,128)(2,1)} %all-gather.2.cloned.1.call-done, s32[4096]{0:T(1024)S(1)} %get-tuple-element.68), kind=kCustom, calls=%fused_computation.2 | custom fusion | bytes 16793600 | tf_op jit(solution)/shard_map/gather | solution.py:69
  252.1 44.1 %subtract_convert_fusion = bf16[4096,4096]{1,0:T(8,128)(2,1)} fusion(bf16[4096,4096]{1,0:T(8,128)(2,1)} %param.11, bf16[4096,1024]{1,0:T(8,128)(2,1)} %gather_fusion.2, bf16[4096,1024]{1,0:T(8,128)(2,1)} %gather_fusion.3), kind=kOutput, calls=%fused_computation.4 | convolution fusion | flops 34410070016 | bytes 83886080 | tf_op jit(solution)/shard_map/dot_general | solution.py:95
  (55 shorter events, 1.9 us)
Async XLA Ops:
  13.1 2.2 copy-start.4
  38.2 5.4 %copy-start = (bf16[1024,1024]{1,0:T(8,128)(2,1)}, bf16[1024,1024]{1,0:T(8,128)(2,1)S(1)}, u32[]{:S(2)}) copy-start(bf16[1024,1024]{1,0:T(8,128)(2,1)S(1)} %copy.11) | copy-start | bytes 6291460
  43.5 5.4 %copy-start.1 = (bf16[1024,1024]{1,0:T(8,128)(2,1)S(1)}, bf16[1024,1024]{1,0:T(8,128)(2,1)}, u32[]{:S(2)}) copy-start(bf16[1024,1024]{1,0:T(8,128)(2,1)} %gather_fusion) | copy-start | bytes 6291460
  43.5 32.7 %all-to-all-start = ((bf16[8,128,1024]{2,1,0:T(8,128)(2,1)}), bf16[8,128,1024]{2,1,0:T(8,128)(2,1)}, u32[]{:S(2)}, u32[]{:S(2)}) async-start(bf16[8,128,1024]{2,1,0:T(8,128)(2,1)} %bitcast.82), calls=%async_computation | async-start | bytes 4194304 | tf_op jit(solution)/shard_map/all_to_all | solution.py:90
  48.8 177.9 %all-gather.2.cloned.1.call-start = ((), (), s32[]{:S(2)}) async-start(), calls=%async_computation.2 | async-start | bytes 10485760 | tf_op jit(solution)/shard_map/all_gather | solution.py:92
  49.1 11.5 %collective-permute-start.2 = (bf16[128,1024]{1,0:T(8,128)(2,1)S(1)}, bf16[128,1024]{1,0:T(8,128)(2,1)S(1)}, u32[]{:S(2)}, u32[]{:S(2)}) collective-permute-start(bf16[128,1024]{1,0:T(8,128)(2,1)S(1)} %get-tuple-element.21), channel_id=1, source_target_pairs={{0,3},{1,2},{2,1},{3,0},{4,7},{5,6},{6,5},{7,4},{8,11},{9,10},{10,... | collective-permute-start | bytes 786440 | tf_op jit(solution)/shard_map/ppermute | solution.py:42
  53.4 22.8 %collective-permute-start.1 = (bf16[128,1024]{1,0:T(8,128)(2,1)S(1)}, bf16[128,1024]{1,0:T(8,128)(2,1)S(1)}, u32[]{:S(2)}, u32[]{:S(2)}) collective-permute-start(bf16[128,1024]{1,0:T(8,128)(2,1)S(1)} %get-tuple-element.22), channel_id=1, source_target_pairs={{0,2},{1,3},{2,0},{3,1},{4,6},{5,7},{6,4},{7,5},{8,10},{9,11},{10,... | collective-permute-start | bytes 786440 | tf_op jit(solution)/shard_map/ppermute | solution.py:42
  53.4 22.8 %collective-permute-start = (bf16[128,1024]{1,0:T(8,128)(2,1)S(1)}, bf16[128,1024]{1,0:T(8,128)(2,1)S(1)}, u32[]{:S(2)}, u32[]{:S(2)}) collective-permute-start(bf16[128,1024]{1,0:T(8,128)(2,1)S(1)} %get-tuple-element.23), channel_id=1, source_target_pairs={{0,1},{1,0},{2,3},{3,2},{4,5},{5,4},{6,7},{7,6},{8,9},{9,8},{10,11... | collective-permute-start | bytes 786440 | tf_op jit(solution)/shard_map/ppermute | solution.py:42
  76.3 27.1 %collective-permute-start.8 = (bf16[512,1024]{1,0:T(8,128)(2,1)S(1)}, bf16[512,1024]{1,0:T(8,128)(2,1)S(1)}, u32[]{:S(2)}, u32[]{:S(2)}) collective-permute-start(bf16[512,1024]{1,0:T(8,128)(2,1)S(1)} %pad_maximum_fusion.1), channel_id=1, source_target_pairs={{0,24},{4,28},{8,16},{12,20},{16,8},{20,12},{24,0},{28,4},{1,25},{... | collective-permute-start | bytes 3145736 | tf_op jit(solution)/shard_map/ppermute | solution.py:42
  79.0 45.3 %collective-permute-start.7 = (bf16[512,1024]{1,0:T(8,128)(2,1)S(1)}, bf16[512,1024]{1,0:T(8,128)(2,1)S(1)}, u32[]{:S(2)}, u32[]{:S(2)}) collective-permute-start(bf16[512,1024]{1,0:T(8,128)(2,1)S(1)} %pad_maximum_fusion.1), channel_id=1, source_target_pairs={{0,16},{4,20},{8,24},{12,28},{16,0},{20,4},{24,8},{28,12},{1,17},{... | collective-permute-start | bytes 3145736 | tf_op jit(solution)/shard_map/ppermute | solution.py:42
  79.5 44.9 %collective-permute-start.6 = (bf16[512,1024]{1,0:T(8,128)(2,1)S(1)}, bf16[512,1024]{1,0:T(8,128)(2,1)S(1)}, u32[]{:S(2)}, u32[]{:S(2)}) collective-permute-start(bf16[512,1024]{1,0:T(8,128)(2,1)S(1)} %pad_maximum_fusion.1), channel_id=1, source_target_pairs={{0,8},{4,12},{8,0},{12,4},{16,24},{20,28},{24,16},{28,20},{1,9},{5... | collective-permute-start | bytes 3145736 | tf_op jit(solution)/shard_map/ppermute | solution.py:42
  124.4 2.3 copy-start.2
  126.7 48.9 %collective-permute-start.9 = (bf16[2048,1024]{1,0:T(8,128)(2,1)}, bf16[2048,1024]{1,0:T(8,128)(2,1)}, u32[]{:S(2)}, u32[]{:S(2)}) collective-permute-start(bf16[2048,1024]{1,0:T(8,128)(2,1)} %pad_maximum_fusion), channel_id=1, source_target_pairs={{0,4},{4,0},{8,12},{12,8},{16,20},{20,16},{24,28},{28,24},{1,5},{5... | collective-permute-start | bytes 12582920 | tf_op jit(solution)/shard_map/ppermute | solution.py:42
  126.8 21.1 %all-to-all-start.1 = ((s32[8,1,128]{2,1,0:T(1,128)}), s32[8,1,128]{2,1,0:T(1,128)S(1)}, u32[]{:S(2)}, u32[]{:S(2)}) async-start(s32[8,1,128]{2,1,0:T(1,128)} %bitcast.15), calls=%async_computation.1 | async-start | bytes 8192 | tf_op jit(solution)/shard_map/all_to_all | solution.py:81
  130.9 5.4 %collective-permute-start.12 = (s32[128]{0:T(128)S(1)}, s32[128]{0:T(128)S(1)}, u32[]{:S(2)}, u32[]{:S(2)}) collective-permute-start(s32[128]{0:T(128)S(1)} %get-tuple-element.55), channel_id=1, source_target_pairs={{0,3},{1,2},{2,1},{3,0},{4,7},{5,6},{6,5},{7,4},{8,11},{9,10},{10,... | collective-permute-start | bytes 1544 | tf_op jit(solution)/shard_map/ppermute | solution.py:42
  133.5 5.9 %collective-permute-start.11 = (s32[128]{0:T(128)S(1)}, s32[128]{0:T(128)S(1)}, u32[]{:S(2)}, u32[]{:S(2)}) collective-permute-start(s32[128]{0:T(128)S(1)} %get-tuple-element.56), channel_id=1, source_target_pairs={{0,2},{1,3},{2,0},{3,1},{4,6},{5,7},{6,4},{7,5},{8,10},{9,11},{10,... | collective-permute-start | bytes 1544 | tf_op jit(solution)/shard_map/ppermute | solution.py:42
  133.5 5.9 %collective-permute-start.10 = (s32[128]{0:T(128)S(1)}, s32[128]{0:T(128)S(1)}, u32[]{:S(2)}, u32[]{:S(2)}) collective-permute-start(s32[128]{0:T(128)S(1)} %get-tuple-element.57), channel_id=1, source_target_pairs={{0,1},{1,0},{2,3},{3,2},{4,5},{5,4},{6,7},{7,6},{8,9},{9,8},{10,11... | collective-permute-start | bytes 1544 | tf_op jit(solution)/shard_map/ppermute | solution.py:42
  139.5 12.9 %collective-permute-start.15 = (s32[512]{0:T(512)S(1)}, s32[512]{0:T(512)S(1)}, u32[]{:S(2)}, u32[]{:S(2)}) collective-permute-start(s32[512]{0:T(512)S(1)} %pad_add_fusion.1), channel_id=1, source_target_pairs={{0,24},{4,28},{8,16},{12,20},{16,8},{20,12},{24,0},{28,4},{1,25},{... | collective-permute-start | bytes 6152 | tf_op jit(solution)/shard_map/ppermute | solution.py:42
  142.3 5.5 %collective-permute-start.14 = (s32[512]{0:T(512)S(1)}, s32[512]{0:T(512)S(1)}, u32[]{:S(2)}, u32[]{:S(2)}) collective-permute-start(s32[512]{0:T(512)S(1)} %pad_add_fusion.1), channel_id=1, source_target_pairs={{0,16},{4,20},{8,24},{12,28},{16,0},{20,4},{24,8},{28,12},{1,17},{... | collective-permute-start | bytes 6152 | tf_op jit(solution)/shard_map/ppermute | solution.py:42
  144.3 3.6 %collective-permute-start.13 = (s32[512]{0:T(512)S(1)}, s32[512]{0:T(512)S(1)}, u32[]{:S(2)}, u32[]{:S(2)}) collective-permute-start(s32[512]{0:T(512)S(1)} %pad_add_fusion.1), channel_id=1, source_target_pairs={{0,8},{4,12},{8,0},{12,4},{16,24},{20,28},{24,16},{28,20},{1,9},{5... | collective-permute-start | bytes 6152 | tf_op jit(solution)/shard_map/ppermute | solution.py:42
  147.9 5.6 %collective-permute-start.5 = (s32[1024]{0:T(1024)S(1)}, s32[1024]{0:T(1024)S(1)}, u32[]{:S(2)}, u32[]{:S(2)}) collective-permute-start(s32[1024]{0:T(1024)S(1)} %bitcast.87), channel_id=1, source_target_pairs={{0,3},{1,2},{2,1},{3,0},{4,7},{5,6},{6,5},{7,4},{8,11},{9,10},{10,... | collective-permute-start | bytes 12296 | tf_op jit(solution)/shard_map/ppermute | solution.py:42
  148.6 4.9 %collective-permute-start.4 = (s32[1024]{0:T(1024)S(1)}, s32[1024]{0:T(1024)S(1)}, u32[]{:S(2)}, u32[]{:S(2)}) collective-permute-start(s32[1024]{0:T(1024)S(1)} %bitcast.88), channel_id=1, source_target_pairs={{0,2},{1,3},{2,0},{3,1},{4,6},{5,7},{6,4},{7,5},{8,10},{9,11},{10,... | collective-permute-start | bytes 12296 | tf_op jit(solution)/shard_map/ppermute | solution.py:42
  148.6 10.1 %collective-permute-start.3 = (s32[1024]{0:T(1024)S(1)}, s32[1024]{0:T(1024)S(1)}, u32[]{:S(2)}, u32[]{:S(2)}) collective-permute-start(s32[1024]{0:T(1024)S(1)} %bitcast.89), channel_id=1, source_target_pairs={{0,1},{1,0},{2,3},{3,2},{4,5},{5,4},{6,7},{7,6},{8,9},{9,8},{10,11... | collective-permute-start | bytes 12296 | tf_op jit(solution)/shard_map/ppermute | solution.py:42
  152.4 12.8 %collective-permute-start.16 = (s32[2048]{0:T(1024)S(1)}, s32[2048]{0:T(1024)S(1)}, u32[]{:S(2)}, u32[]{:S(2)}) collective-permute-start(s32[2048]{0:T(1024)S(1)} %get-tuple-element.49), channel_id=1, source_target_pairs={{0,4},{4,0},{8,12},{12,8},{16,20},{20,16},{24,28},{28,24},{1,5},{5... | collective-permute-start | bytes 24584 | tf_op jit(solution)/shard_map/ppermute | solution.py:42
  170.9 1.6 copy-start.3
Sparse Core Ops, SparseCore 0:
  76.4 150.2 all-gather.1
